TPU v7x, 256 devices: a whole 4x4x8 slice. The times are simulated.
256 devices in a mesh: rows: 4 (over x), chan: 8 (over y, z_lo), filt: 8 (over z_hi, core).
Axes of the slice: x: 4, y: 4, z: 8 (z_hi: 4, z_lo: 2; z = z_hi * 2 + z_lo), core: 2. Of those that a mesh axis runs over, the one named last changes fastest.
Arguments:
- images: bfloat16 [16, 2048, 2048], P('rows', 'chan', 'filt'), may hold values from -6 to 6
- first_weight: bfloat16 [2048, 1024], P('chan', 'filt'), may hold values from -0.125 to 0.125
- group_weight: bfloat16 [3, 3, 32, 1024], P(None, None, None, 'filt'), may hold values from -0.375 to 0.375
- third_weight: bfloat16 [1024, 2048], P('chan', 'filt'), may hold values from -0.1875 to 0.1875
- out_grad: bfloat16 [16, 2048, 2048], P('rows', 'chan', 'filt'), may hold values from -6 to 6
Outputs:
- block_out: bfloat16 [16, 2048, 2048], P('rows', 'chan', 'filt')
- images_grad: float32 [16, 2048, 2048], P('rows', 'chan', 'filt')
- first_grad: float32 [2048, 1024], P('chan', 'filt')
- group_grad: float32 [3, 3, 32, 1024], P(None, None, None, 'filt')
- third_grad: float32 [1024, 2048], P('chan', 'filt')
All inputs are finite; a program needn't handle non-finite values.
Results may differ from a plain program's by a relative error of at most 0.006.
Values may be sent and summed in bfloat16 or wider, within the bound.
No kernel may reach another device: no remote copies, remote signals or barrier semaphores. Data moves between devices by JAX's collectives and lax.ppermute only.
A program may use at most 128 MiB of HBM per device.

v0:
```python
import jax
import jax.numpy as jnp
from jax import lax
from jax.sharding import PartitionSpec as P


def extended(block, sides, width):
    for axis, dim in sides:
        count = lax.axis_size(axis)
        forward = [(i, i + 1) for i in range(count - 1)]
        backward = [(target, source) for source, target in forward]
        low = lax.ppermute(
            lax.slice_in_dim(block, block.shape[dim] - width, None, axis=dim), axis, forward
        )
        high = lax.ppermute(lax.slice_in_dim(block, 0, width, axis=dim), axis, backward)
        block = jnp.concatenate([low, block, high], axis=dim)
    return block


def silu_slope(values):
    logistic = jax.nn.sigmoid(values)
    return logistic * (1.0 + values * (1.0 - logistic))


def group_conv(padded, kernel, groups_here):
    result = lax.conv_general_dilated(
        padded[None],
        kernel,
        (1, 1),
        "VALID",
        dimension_numbers=("NHWC", "HWIO", "NHWC"),
        feature_group_count=groups_here,
        preferred_element_type=jnp.float32,
    )
    return result[0]


def transposed_kernel(kernel, group_size, groups_here):
    pieces = kernel.reshape(3, 3, group_size, groups_here, group_size)
    swapped = jnp.transpose(pieces, (0, 1, 4, 3, 2)).reshape(
        3, 3, group_size, groups_here * group_size
    )
    return swapped[::-1, ::-1]


def kernel_partial(padded_first, group_delta, group_size, groups_here):
    rows_here = group_delta.shape[0]
    cols_here = group_delta.shape[1]
    pixels = rows_here * cols_here
    delta_groups = group_delta.reshape(pixels, groups_here, group_size)
    kernel_terms = []
    for row_shift in range(3):
        for col_shift in range(3):
            window = padded_first[
                row_shift : row_shift + rows_here, col_shift : col_shift + cols_here
            ]
            window = window.reshape(pixels, groups_here, group_size)
            kernel_terms.append(
                jnp.einsum("pgi,pgo->gio", window, delta_groups, preferred_element_type=jnp.float32)
            )
    kernel_part = jnp.stack(kernel_terms).reshape(3, 3, groups_here, group_size, group_size)
    kernel_part = jnp.transpose(kernel_part, (0, 1, 3, 2, 4))
    return kernel_part.reshape(3, 3, group_size, groups_here * group_size)


def body(images, first_weight, group_weight, third_weight, out_grad):
    rows_here = images.shape[0]
    cols_here = images.shape[1]
    group_size = group_weight.shape[2]
    first_panel, third_panel = (
        lax.all_gather(first_weight, "chan", axis=0, tiled=True),
        lax.all_gather(third_weight, "chan", axis=0, tiled=True),
    )
    pixels = rows_here * cols_here
    groups_here = group_weight.shape[3] // group_size
    gathered = lax.all_gather(images, "filt", axis=2, tiled=True)
    flat_images = gathered.reshape(pixels, gathered.shape[2])
    pre_first = jnp.dot(flat_images, first_panel, preferred_element_type=jnp.float32)
    act_first = (
        jax.nn.silu(pre_first)
        .astype(jnp.bfloat16)
        .reshape(rows_here, cols_here, first_panel.shape[1])
    )
    padded_first = extended(act_first, (("rows", 0), ("chan", 1)), 1)
    pre_group = group_conv(padded_first, group_weight, groups_here)
    act_group = jax.nn.silu(pre_group).astype(jnp.bfloat16)
    mid_whole = lax.all_gather(act_group, "filt", axis=2, tiled=True)
    flat_mid = mid_whole.reshape(pixels, mid_whole.shape[2])
    third_out = jnp.dot(flat_mid, third_panel, preferred_element_type=jnp.float32)
    own_images = images.reshape(pixels, images.shape[2]).astype(jnp.float32)
    block_out = (own_images + third_out).astype(jnp.bfloat16).reshape(images.shape)
    grad_flat = out_grad.reshape(pixels, out_grad.shape[2])
    mid_terms = lax.dot_general(
        grad_flat, third_panel, (((1,), (1,)), ((), ())), preferred_element_type=jnp.float32
    )
    mid_grad = lax.psum_scatter(
        mid_terms.reshape(rows_here, cols_here, mid_terms.shape[1]),
        "filt",
        scatter_dimension=2,
        tiled=True,
    )
    third_part = lax.dot_general(
        flat_mid, grad_flat, (((0,), (0,)), ((), ())), preferred_element_type=jnp.float32
    )
    group_delta = (mid_grad * silu_slope(pre_group)).astype(jnp.bfloat16)
    padded_delta = extended(group_delta, (("rows", 0), ("chan", 1)), 1)
    first_back = group_conv(
        padded_delta, transposed_kernel(group_weight, group_size, groups_here), groups_here
    )
    kernel_part = kernel_partial(padded_first, group_delta, group_size, groups_here)
    first_delta = (first_back.reshape(pixels, first_back.shape[2]) * silu_slope(pre_first)).astype(
        jnp.bfloat16
    )
    first_part = lax.dot_general(
        flat_images, first_delta, (((0,), (0,)), ((), ())), preferred_element_type=jnp.float32
    )
    input_terms = lax.dot_general(
        first_delta, first_panel, (((1,), (1,)), ((), ())), preferred_element_type=jnp.float32
    )
    back_images = lax.psum_scatter(
        input_terms.reshape(rows_here, cols_here, input_terms.shape[1]).astype(jnp.bfloat16),
        "filt",
        scatter_dimension=2,
        tiled=True,
    ).astype(jnp.float32)
    images_grad = out_grad.astype(jnp.float32) + back_images
    group_grad = lax.psum(kernel_part, ("rows", "chan"))
    first_total, third_total = lax.psum((first_part, third_part), "rows")
    first_grad, third_grad = (
        lax.psum_scatter(first_total, "chan", scatter_dimension=0, tiled=True),
        lax.psum_scatter(third_total, "chan", scatter_dimension=0, tiled=True),
    )
    return (block_out, images_grad, first_grad, group_grad, third_grad)


def solution(mesh):
    in_specs = (
        P("rows", "chan", "filt"),
        P("chan", "filt"),
        P(None, None, None, "filt"),
        P("chan", "filt"),
        P("rows", "chan", "filt"),
    )
    out_specs = (
        P("rows", "chan", "filt"),
        P("rows", "chan", "filt"),
        P("chan", "filt"),
        P(None, None, None, "filt"),
        P("chan", "filt"),
    )
    return jax.shard_map(body, mesh=mesh, in_specs=in_specs, out_specs=out_specs, check_vma=False)
```

profile of v0, /device:TPU:32, one launch (start us, length us, event | category | flops | bytes accessed | tf_op | source)
XLA Modules:
  0.0 700.0 jit_solution(2654013649618200023)
XLA Ops:
  7.9 39.6 %all_gather.15 = bf16[1024,256]{1,0:T(8,128)(2,1)S(1)} all-gather(bf16[128,256]{1,0:T(8,128)(2,1)} %param.8), channel_id=1, replica_groups=mesh['rows'=4,'chan'=8,'filt'=8] {'chan'}, dimensions={0}, use_global_device_ids=true | all-gather | bytes 589824 | tf_op jit(solution)/shard_map/all_gather | solution.py:72
  47.5 3.8 fusion.10
  52.2 36.9 %all_gather.13 = bf16[2048,128]{1,0:T(8,128)(2,1)S(1)} all-gather(bf16[256,128]{1,0:T(8,128)(2,1)S(1)} %copy-done.13), channel_id=1, replica_groups=mesh['rows'=4,'chan'=8,'filt'=8] {'chan'}, dimensions={0}, use_global_device_ids=true | all-gather | bytes 589824 | tf_op jit(solution)/shard_map/all_gather | solution.py:71
  89.1 4.4 multiply_convert_fusion.3
  93.5 2.9 collective-permute-start
  96.4 1.3 collective-permute-start.1
  98.4 4.2 collective-permute-done.1
  103.2 3.4 collective-permute-start.2
  106.6 3.2 collective-permute-start.3
  110.7 8.0 %collective-permute-done.2 = bf16[6,1,128]{1,2,0:T(8,128)(2,1)S(1)} collective-permute-done((bf16[6,1,128]{1,2,0:T(8,128)(2,1)S(1)}, bf16[6,1,128]{1,2,0:T(8,128)(2,1)S(1)}, u32[]{:S(2)}, u32[]{:S(2)}) %collective-permute-start.2) | collective-permute-done | bytes 1568 | tf_op jit(solution)/shard_map/ppermute | solution.py:12
  118.7 10.6 %collective-permute-done.3 = bf16[6,1,128]{1,2,0:T(8,128)(2,1)S(1)} collective-permute-done((bf16[6,1,128]{1,2,0:T(8,128)(2,1)S(1)}, bf16[6,1,128]{1,2,0:T(8,128)(2,1)S(1)}, u32[]{:S(2)}, u32[]{:S(2)}) %collective-permute-start.3) | collective-permute-done | bytes 1568 | tf_op jit(solution)/shard_map/ppermute | solution.py:15
  130.0 5.8 copy.36
  135.8 9.4 %fusion.13 = f32[1,4,256,4,32]{4,0,3,2,1:T(1,128)S(1)} fusion(bf16[1,6,258,4,32]{4,0,3,2,1:T(2,128)(2,1)} %copy.36, bf16[3,3,32,4,32]{4,3,2,1,0:T(4,128)(2,1)} %shard_map.94), kind=kOutput, calls=%fused_computation.39 | convolution fusion | flops 75497472 | bytes 994304 | tf_op jit(solution)/shard_map/conv_general_dilated | solution.py:26
  145.3 3.5 copy.38
  148.8 1.3 copy.40
  150.2 2.0 multiply_convert_fusion.1
  152.2 3.3 collective-permute-start.4
  155.6 1.3 collective-permute-start.5
  157.5 4.3 collective-permute-done.5
  161.8 3.5 collective-permute-start.6
  165.3 2.6 collective-permute-start.7
  169.2 2.5 collective-permute-done.7
  172.1 5.9 copy.44
  178.0 13.8 %convolution_reduce_fusion = f32[4,256,4,32]{3,2,1,0:T(4,128)S(1)} fusion(bf16[1,6,258,4,32]{4,0,3,2,1:T(2,128)(2,1)} %copy.44, bf16[3,3,32,4,32]{4,3,2,1,0:T(4,128)(2,1)} %rev.6), kind=kOutput, calls=%fused_computation.2 | convolution fusion | flops 75497472 | bytes 994304 | tf_op jit(solution)/shard_map/conv_general_dilated | solution.py:26
  191.8 1.7 reshape.99
  193.5 1.4 multiply_convert_fusion
  194.9 4.0 convolution_bitcast_fusion
  199.0 3.4 convolution_bitcast_fusion.1
  202.4 40.0 %reduce-scatter.9.cloned.1.call-done = f32[256,128]{0,1:T(8,128)} async-done(((f32[2048,128]{0,1:T(8,128)}), f32[256,128]{0,1:T(8,128)}) %reduce-scatter.9.cloned.1.call-update) | async-done | bytes 131088 | tf_op jit(solution)/shard_map/reduce_scatter | solution.py:130
  242.4 44.5 %reduce-scatter.11.cloned.1.call-done = f32[128,256]{1,0:T(8,128)} async-done(((f32[1024,256]{1,0:T(8,128)}), f32[128,256]{1,0:T(8,128)}) %reduce-scatter.11.cloned.1.call-update) | async-done | bytes 131088 | tf_op jit(solution)/shard_map/reduce_scatter | solution.py:131
  286.9 3.2 convolution_convert_fusion
  291.8 1.2 pad_maximum_fusion.1
  294.3 1.8 reshape.85
  297.0 1.1 reshape.88
  299.1 1.8 reshape.89
  302.2 1.1 reshape.91
  304.2 1.1 reshape.93
  306.2 1.1 reshape.86
  307.3 1.1 fusion.9
  308.9 1.2 fusion.6
  311.5 0.9 reshape.95
  312.5 3.2 fusion
  315.6 21.3 %all-reduce.6.cloned.1.call-done = (f32[256,128]{0,1:T(8,128)}, f32[128,256]{1,0:T(8,128)}) async-done(((f32[256,128]{0,1:T(8,128)}, f32[128,256]{1,0:T(8,128)}), (f32[256,128]{0,1:T(8,128)}, f32[128,256]{1,0:T(8,128)})) %all-reduce.6.cloned.1.call-update) | async-done | bytes 262160 | tf_op jit(solution)/shard_map/psum | solution.py:128
  337.0 1.7 copy.60
  338.7 59.3 %reduce-scatter.7.cloned.1.call-done = bf16[4,256,256]{2,1,0:T(8,128)(2,1)} async-done(((bf16[4,256,2048]{2,1,0:T(8,128)(2,1)}), bf16[4,256,256]{2,1,0:T(8,128)(2,1)}) %reduce-scatter.7.cloned.1.call-update) | async-done | bytes 524304 | tf_op jit(solution)/shard_map/reduce_scatter | solution.py:120
  398.0 2.1 convert_add_fusion
  400.1 290.7 %all-reduce.4.cloned.1.call-done = f32[3,3,32,128]{3,2,1,0:T(8,128)} async-done(((f32[3,3,32,128]{3,2,1,0:T(8,128)}), f32[3,3,32,128]{3,2,1,0:T(8,128)}) %all-reduce.4.cloned.1.call-update) | async-done | bytes 147472 | tf_op jit(solution)/shard_map/psum | solution.py:127
  690.9 1.6 copy.78
  (90 shorter events, 17.4 us)
Async XLA Ops:
  7.2 81.9 %all-gather.3.cloned.1.call-start = ((), (), s32[]{:S(2)}) async-start(), calls=%async_computation.4 | async-start | bytes 4718592 | tf_op jit(solution)/shard_map/all_gather | solution.py:76
  7.9 142.2 %reduce-scatter.5.cloned.1.call-start = ((), (), s32[]{:S(2)}) async-start(), calls=%async_computation.6 | async-start | bytes 4718592 | tf_op jit(solution)/shard_map/reduce_scatter | solution.py:96
  51.3 0.8 copy-start.13
  51.4 147.6 %all-gather.5.cloned.1.call-start = ((), (), s32[]{:S(2)}) async-start(), calls=%async_computation.5 | async-start | bytes 2359296 | tf_op jit(solution)/shard_map/all_gather | solution.py:87
  89.1 4.4 copy-start
  93.5 16.3 %copy-start.12 = (bf16[3,3,32,128]{3,2,1,0:T(8,128)(2,1)S(1)}, bf16[3,3,32,128]{3,2,1,0:T(8,128)(2,1)}, u32[]{:S(2)}) copy-start(bf16[3,3,32,128]{3,2,1,0:T(8,128)(2,1)} %param.7) | copy-start | bytes 221188
  93.5 4.8 collective-permute-start
  96.4 6.2 collective-permute-start.1
  98.3 4.6 copy-start.7
  102.6 0.6 copy-start.9
  103.2 15.5 %collective-permute-start.2 = (bf16[6,1,128]{1,2,0:T(8,128)(2,1)S(1)}, bf16[6,1,128]{1,2,0:T(8,128)(2,1)S(1)}, u32[]{:S(2)}, u32[]{:S(2)}) collective-permute-start(bf16[6,1,128]{1,2,0:T(8,128)(2,1)S(1)} %get-tuple-element.29), channel_id=1, source_target_pairs={{0,8},{8,16},{16,24},{24,32},{32,40},{40,48},{48,56},{1,9},{9,17},... | collective-permute-start | bytes 4616 | tf_op jit(solution)/shard_map/ppermute | solution.py:12
  106.6 22.7 %collective-permute-start.3 = (bf16[6,1,128]{1,2,0:T(8,128)(2,1)S(1)}, bf16[6,1,128]{1,2,0:T(8,128)(2,1)S(1)}, u32[]{:S(2)}, u32[]{:S(2)}) collective-permute-start(bf16[6,1,128]{1,2,0:T(8,128)(2,1)S(1)} %get-tuple-element.30), channel_id=1, source_target_pairs={{8,0},{16,8},{24,16},{32,24},{40,32},{48,40},{56,48},{9,1},{17,9},... | collective-permute-start | bytes 4616 | tf_op jit(solution)/shard_map/ppermute | solution.py:15
  118.7 17.1 %copy-start.4 = (bf16[6,1,128]{1,2,0:T(8,128)(2,1)}, bf16[6,1,128]{1,2,0:T(8,128)(2,1)S(1)}, u32[]{:S(2)}) copy-start(bf16[6,1,128]{1,2,0:T(8,128)(2,1)S(1)} %collective-permute-done.2) | copy-start | bytes 4612
  129.3 0.7 copy-start.6
  148.8 19.0 %copy-start.3 = (bf16[3,3,32,4,32]{4,3,2,1,0:T(4,128)(2,1)S(1)}, bf16[3,3,32,4,32]{4,3,2,1,0:T(4,128)(2,1)}, u32[]{:S(2)}) copy-start(bf16[3,3,32,4,32]{4,3,2,1,0:T(4,128)(2,1)} %shard_map.94) | copy-start | bytes 221188
  152.2 90.2 %reduce-scatter.9.cloned.1.call-start = ((), (), s32[]{:S(2)}) async-start(), calls=%async_computation.9 | async-start | bytes 1179648 | tf_op jit(solution)/shard_map/reduce_scatter | solution.py:130
  152.2 5.2 collective-permute-start.4
  155.6 6.2 collective-permute-start.5
  161.8 7.4 %collective-permute-start.6 = (bf16[6,1,128]{2,1,0:T(2,128)(2,1)S(1)}, bf16[6,1,128]{2,1,0:T(2,128)(2,1)S(1)}, u32[]{:S(2)}, u32[]{:S(2)}) collective-permute-start(bf16[6,1,128]{2,1,0:T(2,128)(2,1)S(1)} %get-tuple-element.27), channel_id=1, source_target_pairs={{0,8},{8,16},{16,24},{24,32},{32,40},{40,48},{48,56},{1,9},{9,17},... | collective-permute-start | bytes 4616 | tf_op jit(solution)/shard_map/ppermute | solution.py:12
  165.3 6.4 collective-permute-start.7
  194.9 4.1 copy-start.2
  198.9 88.0 %copy-start.1 = (bf16[2048,128]{1,0:T(8,128)(2,1)S(1)}, bf16[2048,128]{1,0:T(8,128)(2,1)}, u32[]{:S(2)}) copy-start(bf16[2048,128]{1,0:T(8,128)(2,1)} %copy-done) | copy-start | bytes 1572868
  198.9 88.0 %reduce-scatter.11.cloned.1.call-start = ((), (), s32[]{:S(2)}) async-start(), calls=%async_computation.10 | async-start | bytes 1179648 | tf_op jit(solution)/shard_map/reduce_scatter | solution.py:131
  202.4 134.6 %all-reduce.6.cloned.1.call-start = ((), (), s32[]{:S(2)}) async-start(), calls=%async_computation.11 | async-start | bytes 524288 | tf_op jit(solution)/shard_map/psum | solution.py:128
  286.9 111.1 %reduce-scatter.7.cloned.1.call-start = ((), (), s32[]{:S(2)}) async-start(), calls=%async_computation.7 | async-start | bytes 4718592 | tf_op jit(solution)/shard_map/reduce_scatter | solution.py:120
  290.2 0.8 copy-start.8
  290.2 0.9 copy-start.10
  290.2 1.6 copy-start.5
  290.2 400.7 %all-reduce.4.cloned.1.call-start = ((), (), s32[]{:S(2)}) async-start(), calls=%async_computation.8 | async-start | bytes 294912 | tf_op jit(solution)/shard_map/psum | solution.py:127
  337.0 355.5 %copy-start.11 = (f32[128,256]{1,0:T(8,128)S(1)}, f32[128,256]{1,0:T(8,128)}, u32[]{:S(2)}) copy-start(f32[128,256]{1,0:T(8,128)} %get-tuple-element.46) | copy-start | bytes 393220
Sparse Core Ops, SparseCore 0:
  9.8 60.3 all-gather.2
  72.7 76.7 reduce-scatter.4
  152.3 42.8 all-gather.4
  199.0 43.3 reduce-scatter.8
  244.8 42.0 reduce-scatter.10
  289.1 47.8 all-reduce.5
  339.7 58.2 reduce-scatter.6
  401.4 289.4 all-reduce.3
where the time goes:
time: 701 us; the launch traced here: 700 us
  waiting for transfers between devices  487 us (69%)
  blocking collectives  76.5 us (11%)
  matrix products  49 us (7%)
  local copies, waits for them, and re-layouts  43.4 us (6%)
  starting transfers between devices  22 us (3%)
  between operations  14.5 us (2%)
  other arithmetic  7.29 us (1%)
    psum x1, waiting for transfers between devices, body(): group_grad = lax.psum(kernel_part, ('rows', 'chan'))  291 us
    reduce_scatter x1, waiting for transfers between devices, body(): lax.psum_scatter(input_terms.reshape(rows_here, cols_here, input_terms.sh...  59.3 us
    reduce_scatter x1, waiting for transfers between devices, body(): lax.psum_scatter(third_total, 'chan', scatter_dimension=0, tiled=True)  44.5 us
    reduce_scatter x1, waiting for transfers between devices, body(): lax.psum_scatter(first_total, 'chan', scatter_dimension=0, tiled=True)  40 us
    all_gather x1, blocking collectives, body(): lax.all_gather(third_weight, 'chan', axis=0, tiled=True)  39.6 us
    all_gather x1, blocking collectives, body(): lax.all_gather(first_weight, 'chan', axis=0, tiled=True)  36.9 us
    conv_general_dilated x2, matrix products, group_conv(): lax.conv_general_dilated(padded[None], kernel, (1, 1), 'VALID', dimension...  23.3 us
    ppermute x4, waiting for transfers between devices, extended(): lax.ppermute(lax.slice_in_dim(block, 0, width, axis=dim), axis, backward)  21.5 us
  transfers between devices with their start and end apart: 16, of which 12 were waited for; matrix products, arithmetic and copies ran while one was open for 13% of the time, Pallas kernels for 0%

commit v1 on v0

--- a/solution.py
+++ b/solution.py
@@ -124,7 +124,7 @@
         tiled=True,
     ).astype(jnp.float32)
     images_grad = out_grad.astype(jnp.float32) + back_images
-    group_grad = lax.psum(kernel_part, ("rows", "chan"))
+    group_grad = jnp.sum(lax.all_gather(kernel_part, ("rows", "chan")), axis=0)
     first_total, third_total = lax.psum((first_part, third_part), "rows")
     first_grad, third_grad = (
         lax.psum_scatter(first_total, "chan", scatter_dimension=0, tiled=True),

time: 701 us -> 586 us (0.84)
  waiting for transfers between devices: 487 us -> 375 us
    psum x1 -> x0, waiting for transfers between devices: 291 us -> none  [body(): group_grad = lax.psum(kernel_part, ('rows', 'chan'))]
    all_gather x0 -> x1, waiting for transfers between devices: none -> 174 us  [body(): group_grad = jnp.sum(lax.all_gather(kernel_part, ('rows', 'chan')), axis=0)]
  transfers between devices with their start and end apart: 16 -> 16, of which waited for: 12 -> 12; matrix products, arithmetic and copies ran while one was open for 13% -> 15% of each run, Pallas kernels for 0% -> 0%
where the time goes in v1:
time: 586 us; the launch traced here: 585 us
  waiting for transfers between devices  375 us (64%)
  blocking collectives  76.5 us (13%)
  matrix products  49 us (8%)
  local copies, waits for them, and re-layouts  39.2 us (7%)
  starting transfers between devices  20.8 us (4%)
  between operations  14.5 us (2%)
  other arithmetic  9.81 us (2%)
    all_gather x1, waiting for transfers between devices, body(): group_grad = jnp.sum(lax.all_gather(kernel_part, ('rows', 'chan')), axis=0)  174 us
    reduce_scatter x1, waiting for transfers between devices, body(): lax.psum_scatter(input_terms.reshape(rows_here, cols_here, input_terms.sh...  59.4 us
    reduce_scatter x1, waiting for transfers between devices, body(): lax.psum_scatter(third_total, 'chan', scatter_dimension=0, tiled=True)  44.3 us
    reduce_scatter x1, waiting for transfers between devices, body(): lax.psum_scatter(first_total, 'chan', scatter_dimension=0, tiled=True)  40 us
    all_gather x1, blocking collectives, body(): lax.all_gather(third_weight, 'chan', axis=0, tiled=True)  39.6 us
    all_gather x1, blocking collectives, body(): lax.all_gather(first_weight, 'chan', axis=0, tiled=True)  36.9 us
    psum x1, waiting for transfers between devices, body(): first_total, third_total = lax.psum((first_part, third_part), 'rows')  24.9 us
    conv_general_dilated x2, matrix products, group_conv(): lax.conv_general_dilated(padded[None], kernel, (1, 1), 'VALID', dimension...  23.3 us
  transfers between devices with their start and end apart: 16, of which 12 were waited for; matrix products, arithmetic and copies ran while one was open for 15% of the time, Pallas kernels for 0%

profile of v1, /device:TPU:32, one launch (start us, length us, event | category | flops | bytes accessed | tf_op | source)
XLA Modules:
  0.0 584.7 jit_solution(12277533981861192721)
XLA Ops:
  7.9 39.6 %all_gather.18 = bf16[1024,256]{1,0:T(8,128)(2,1)S(1)} all-gather(bf16[128,256]{1,0:T(8,128)(2,1)} %param.8), channel_id=1, replica_groups=mesh['rows'=4,'chan'=8,'filt'=8] {'chan'}, dimensions={0}, use_global_device_ids=true | all-gather | bytes 589824 | tf_op jit(solution)/shard_map/all_gather | solution.py:72
  47.5 3.8 fusion.10
  52.2 36.9 %all_gather.16 = bf16[2048,128]{1,0:T(8,128)(2,1)S(1)} all-gather(bf16[256,128]{1,0:T(8,128)(2,1)S(1)} %copy-done.16), channel_id=1, replica_groups=mesh['rows'=4,'chan'=8,'filt'=8] {'chan'}, dimensions={0}, use_global_device_ids=true | all-gather | bytes 589824 | tf_op jit(solution)/shard_map/all_gather | solution.py:71
  89.1 4.4 multiply_convert_fusion.3
  93.5 2.9 collective-permute-start
  96.4 1.3 collective-permute-start.1
  98.4 4.2 collective-permute-done.1
  103.2 3.4 collective-permute-start.2
  106.6 3.2 collective-permute-start.3
  110.7 8.0 %collective-permute-done.2 = bf16[6,1,128]{1,2,0:T(8,128)(2,1)S(1)} collective-permute-done((bf16[6,1,128]{1,2,0:T(8,128)(2,1)S(1)}, bf16[6,1,128]{1,2,0:T(8,128)(2,1)S(1)}, u32[]{:S(2)}, u32[]{:S(2)}) %collective-permute-start.2) | collective-permute-done | bytes 1568 | tf_op jit(solution)/shard_map/ppermute | solution.py:12
  118.7 11.4 %collective-permute-done.3 = bf16[6,1,128]{1,2,0:T(8,128)(2,1)S(1)} collective-permute-done((bf16[6,1,128]{1,2,0:T(8,128)(2,1)S(1)}, bf16[6,1,128]{1,2,0:T(8,128)(2,1)S(1)}, u32[]{:S(2)}, u32[]{:S(2)}) %collective-permute-start.3) | collective-permute-done | bytes 1568 | tf_op jit(solution)/shard_map/ppermute | solution.py:15
  130.8 5.8 copy.63
  136.6 9.4 %fusion.13 = f32[1,4,256,4,32]{4,0,3,2,1:T(1,128)S(1)} fusion(bf16[1,6,258,4,32]{4,0,3,2,1:T(2,128)(2,1)} %copy.63, bf16[3,3,32,4,32]{4,3,2,1,0:T(4,128)(2,1)} %shard_map.94), kind=kOutput, calls=%fused_computation.40 | convolution fusion | flops 75497472 | bytes 994304 | tf_op jit(solution)/shard_map/conv_general_dilated | solution.py:26
  146.0 3.5 copy.65
  149.6 1.3 copy.67
  150.9 2.0 multiply_convert_fusion.1
  153.0 2.2 collective-permute-start.4
  155.2 1.3 collective-permute-start.5
  157.0 4.3 collective-permute-done.5
  161.3 3.9 collective-permute-start.6
  165.3 2.1 collective-permute-start.7
  168.7 2.9 collective-permute-done.7
  172.1 5.9 %copy.71 = bf16[1,6,258,4,32]{4,0,3,2,1:T(2,128)(2,1)} copy(bf16[1,6,258,4,32]{2,4,3,1,0:T(8,128)(2,1)S(1)} %bitcast.121) | data formatting | bytes 792576 | tf_op jit(solution)/shard_map/broadcast_in_dim | solution.py:27
  177.9 13.8 %convolution_reduce_fusion = f32[4,256,4,32]{3,2,1,0:T(4,128)S(1)} fusion(bf16[1,6,258,4,32]{4,0,3,2,1:T(2,128)(2,1)} %copy.71, bf16[3,3,32,4,32]{4,3,2,1,0:T(4,128)(2,1)} %rev.6), kind=kOutput, calls=%fused_computation.2 | convolution fusion | flops 75497472 | bytes 994304 | tf_op jit(solution)/shard_map/conv_general_dilated | solution.py:26
  191.8 1.7 reshape.95
  193.5 1.4 multiply_convert_fusion
  194.9 4.0 convolution_bitcast_fusion
  199.0 3.4 convolution_bitcast_fusion.1
  202.4 40.0 %reduce-scatter.9.cloned.1.call-done = f32[256,128]{0,1:T(8,128)} async-done(((f32[2048,128]{0,1:T(8,128)}), f32[256,128]{0,1:T(8,128)}) %reduce-scatter.9.cloned.1.call-update) | async-done | bytes 131088 | tf_op jit(solution)/shard_map/reduce_scatter | solution.py:130
  242.4 44.3 %reduce-scatter.11.cloned.1.call-done = f32[128,256]{1,0:T(8,128)} async-done(((f32[1024,256]{1,0:T(8,128)}), f32[128,256]{1,0:T(8,128)}) %reduce-scatter.11.cloned.1.call-update) | async-done | bytes 131088 | tf_op jit(solution)/shard_map/reduce_scatter | solution.py:131
  286.8 3.3 convolution_convert_fusion
  293.1 0.9 copy.75
  294.0 1.8 reshape.82
  297.7 0.9 copy.82
  298.6 1.1 reshape.88
  299.7 0.9 copy.84
  300.6 1.1 reshape.90
  302.6 1.1 reshape.83
  303.7 1.1 fusion.9
  305.3 1.2 fusion.6
  307.9 0.9 all_gather_reshape.3
  308.9 3.1 fusion
  312.0 24.9 %all-reduce.3.cloned.1.call-done = (f32[256,128]{0,1:T(8,128)}, f32[128,256]{1,0:T(8,128)}) async-done(((f32[256,128]{0,1:T(8,128)}, f32[128,256]{1,0:T(8,128)}), (f32[256,128]{0,1:T(8,128)}, f32[128,256]{1,0:T(8,128)})) %all-reduce.3.cloned.1.call-update) | async-done | bytes 262160 | tf_op jit(solution)/shard_map/psum | solution.py:128
  336.9 1.7 copy.87
  338.5 59.4 %reduce-scatter.7.cloned.1.call-done = bf16[4,256,256]{2,1,0:T(8,128)(2,1)} async-done(((bf16[4,256,2048]{2,1,0:T(8,128)(2,1)}), bf16[4,256,256]{2,1,0:T(8,128)(2,1)}) %reduce-scatter.7.cloned.1.call-update) | async-done | bytes 524304 | tf_op jit(solution)/shard_map/reduce_scatter | solution.py:120
  397.9 2.1 convert_add_fusion
  400.0 173.8 %all-gather.8.cloned.1.call-done = f32[32,3,3,32,128]{4,3,2,1,0:T(8,128)} async-done(((f32[1,3,3,32,128]{4,3,2,1,0:T(8,128)}), f32[32,3,3,32,128]{4,3,2,1,0:T(8,128)}) %all-gather.8.cloned.1.call-update) | async-done | bytes 4718608 | tf_op jit(solution)/shard_map/all_gather | solution.py:127
  573.8 3.4 reduce_sum.9
  (96 shorter events, 15.2 us)
Async XLA Ops:
  7.2 81.9 %all-gather.4.cloned.1.call-start = ((), (), s32[]{:S(2)}) async-start(), calls=%async_computation.4 | async-start | bytes 4718592 | tf_op jit(solution)/shard_map/all_gather | solution.py:76
  7.9 143.0 %reduce-scatter.5.cloned.1.call-start = ((), (), s32[]{:S(2)}) async-start(), calls=%async_computation.6 | async-start | bytes 4718592 | tf_op jit(solution)/shard_map/reduce_scatter | solution.py:96
  51.4 0.8 copy-start.16
  51.4 147.6 %all-gather.6.cloned.1.call-start = ((), (), s32[]{:S(2)}) async-start(), calls=%async_computation.5 | async-start | bytes 2359296 | tf_op jit(solution)/shard_map/all_gather | solution.py:87
  89.1 4.4 copy-start
  93.5 16.3 %copy-start.15 = (bf16[3,3,32,128]{3,2,1,0:T(8,128)(2,1)S(1)}, bf16[3,3,32,128]{3,2,1,0:T(8,128)(2,1)}, u32[]{:S(2)}) copy-start(bf16[3,3,32,128]{3,2,1,0:T(8,128)(2,1)} %param.7) | copy-start | bytes 221188
  93.5 4.8 collective-permute-start
  96.4 6.2 %collective-permute-start.1 = (bf16[1,256,128]{2,1,0:T(8,128)(2,1)S(1)}, bf16[1,256,128]{2,1,0:T(8,128)(2,1)S(1)}, u32[]{:S(2)}, u32[]{:S(2)}) collective-permute-start(bf16[1,256,128]{2,1,0:T(8,128)(2,1)S(1)} %get-tuple-element.41), channel_id=1, source_target_pairs={{64,0},{128,64},{192,128},{65,1},{129,65},{193,129},{66,2},{130,66... | collective-permute-start | bytes 196616 | tf_op jit(solution)/shard_map/ppermute | solution.py:15
  98.3 4.6 copy-start.10
  102.6 0.6 copy-start.12
  103.2 15.5 %collective-permute-start.2 = (bf16[6,1,128]{1,2,0:T(8,128)(2,1)S(1)}, bf16[6,1,128]{1,2,0:T(8,128)(2,1)S(1)}, u32[]{:S(2)}, u32[]{:S(2)}) collective-permute-start(bf16[6,1,128]{1,2,0:T(8,128)(2,1)S(1)} %get-tuple-element.34), channel_id=1, source_target_pairs={{0,8},{8,16},{16,24},{24,32},{32,40},{40,48},{48,56},{1,9},{9,17},... | collective-permute-start | bytes 4616 | tf_op jit(solution)/shard_map/ppermute | solution.py:12
  106.6 23.5 %collective-permute-start.3 = (bf16[6,1,128]{1,2,0:T(8,128)(2,1)S(1)}, bf16[6,1,128]{1,2,0:T(8,128)(2,1)S(1)}, u32[]{:S(2)}, u32[]{:S(2)}) collective-permute-start(bf16[6,1,128]{1,2,0:T(8,128)(2,1)S(1)} %get-tuple-element.35), channel_id=1, source_target_pairs={{8,0},{16,8},{24,16},{32,24},{40,32},{48,40},{56,48},{9,1},{17,9},... | collective-permute-start | bytes 4616 | tf_op jit(solution)/shard_map/ppermute | solution.py:15
  118.7 17.9 %copy-start.5 = (bf16[6,1,128]{1,2,0:T(8,128)(2,1)}, bf16[6,1,128]{1,2,0:T(8,128)(2,1)S(1)}, u32[]{:S(2)}) copy-start(bf16[6,1,128]{1,2,0:T(8,128)(2,1)S(1)} %collective-permute-done.2) | copy-start | bytes 4612
  130.1 0.7 copy-start.7
  149.6 17.8 %copy-start.3 = (bf16[3,3,32,4,32]{4,3,2,1,0:T(4,128)(2,1)S(1)}, bf16[3,3,32,4,32]{4,3,2,1,0:T(4,128)(2,1)}, u32[]{:S(2)}) copy-start(bf16[3,3,32,4,32]{4,3,2,1,0:T(4,128)(2,1)} %shard_map.94) | copy-start | bytes 221188
  152.9 89.5 %reduce-scatter.9.cloned.1.call-start = ((), (), s32[]{:S(2)}) async-start(), calls=%async_computation.9 | async-start | bytes 1179648 | tf_op jit(solution)/shard_map/reduce_scatter | solution.py:130
  153.0 4.1 collective-permute-start.4
  155.2 6.2 %collective-permute-start.5 = (bf16[1,256,128]{2,1,0:T(8,128)(2,1)S(1)}, bf16[1,256,128]{2,1,0:T(8,128)(2,1)S(1)}, u32[]{:S(2)}, u32[]{:S(2)}) collective-permute-start(bf16[1,256,128]{2,1,0:T(8,128)(2,1)S(1)} %get-tuple-element.39), channel_id=1, source_target_pairs={{64,0},{128,64},{192,128},{65,1},{129,65},{193,129},{66,2},{130,66... | collective-permute-start | bytes 196616 | tf_op jit(solution)/shard_map/ppermute | solution.py:15
  161.3 7.4 %collective-permute-start.6 = (bf16[6,1,128]{2,1,0:T(2,128)(2,1)S(1)}, bf16[6,1,128]{2,1,0:T(2,128)(2,1)S(1)}, u32[]{:S(2)}, u32[]{:S(2)}) collective-permute-start(bf16[6,1,128]{2,1,0:T(2,128)(2,1)S(1)} %get-tuple-element.32), channel_id=1, source_target_pairs={{0,8},{8,16},{16,24},{24,32},{32,40},{40,48},{48,56},{1,9},{9,17},... | collective-permute-start | bytes 4616 | tf_op jit(solution)/shard_map/ppermute | solution.py:12
  165.3 6.4 %collective-permute-start.7 = (bf16[6,1,128]{2,1,0:T(2,128)(2,1)S(1)}, bf16[6,1,128]{2,1,0:T(2,128)(2,1)S(1)}, u32[]{:S(2)}, u32[]{:S(2)}) collective-permute-start(bf16[6,1,128]{2,1,0:T(2,128)(2,1)S(1)} %get-tuple-element.33), channel_id=1, source_target_pairs={{8,0},{16,8},{24,16},{32,24},{40,32},{48,40},{56,48},{9,1},{17,9},... | collective-permute-start | bytes 4616 | tf_op jit(solution)/shard_map/ppermute | solution.py:15
  194.9 4.1 copy-start.2
  198.9 87.9 %copy-start.1 = (bf16[2048,128]{1,0:T(8,128)(2,1)S(1)}, bf16[2048,128]{1,0:T(8,128)(2,1)}, u32[]{:S(2)}) copy-start(bf16[2048,128]{1,0:T(8,128)(2,1)} %copy-done) | copy-start | bytes 1572868
  198.9 87.8 %reduce-scatter.11.cloned.1.call-start = ((), (), s32[]{:S(2)}) async-start(), calls=%async_computation.10 | async-start | bytes 1179648 | tf_op jit(solution)/shard_map/reduce_scatter | solution.py:131
  202.4 134.5 %all-reduce.3.cloned.1.call-start = ((), (), s32[]{:S(2)}) async-start(), calls=%async_computation.11 | async-start | bytes 524288 | tf_op jit(solution)/shard_map/psum | solution.py:128
  286.8 111.2 %reduce-scatter.7.cloned.1.call-start = ((), (), s32[]{:S(2)}) async-start(), calls=%async_computation.7 | async-start | bytes 4718592 | tf_op jit(solution)/shard_map/reduce_scatter | solution.py:120
  290.1 0.8 copy-start.11
  290.1 0.9 copy-start.13
  290.1 2.3 copy-start.6
  290.1 2.3 copy-start.8
  290.1 283.7 %all-gather.8.cloned.1.call-start = ((), (), s32[]{:S(2)}) async-start(), calls=%async_computation.8 | async-start | bytes 4866048 | tf_op jit(solution)/shard_map/all_gather | solution.py:127
  297.5 7.4 %copy-start.4 = (bf16[1024,4,32]{0,2,1:T(8,128)(2,1)S(1)}, bf16[1024,4,32]{0,2,1:T(8,128)(2,1)}, u32[]{:S(2)}) copy-start(bf16[1024,4,32]{0,2,1:T(8,128)(2,1)} %reshape.84) | copy-start | bytes 786436
  306.7 2.2 copy-start.9
  400.0 177.2 %copy-start.14 = (f32[128,256]{1,0:T(8,128)S(1)}, f32[128,256]{1,0:T(8,128)}, u32[]{:S(2)}) copy-start(f32[128,256]{1,0:T(8,128)} %get-tuple-element.51) | copy-start | bytes 393220
Sparse Core Ops, SparseCore 0:
  9.8 60.3 all-gather.3
  72.7 76.6 reduce-scatter.4
  153.0 42.0 all-gather.5
  199.0 43.3 reduce-scatter.8
  244.8 41.9 reduce-scatter.10
  289.0 47.8 all-reduce.2
  339.6 58.2 reduce-scatter.6
  400.4 173.3 all-gather.7
